TPU v7x, 256 devices: a whole 4x4x8 slice. The times are simulated.
256 devices in a mesh: dp: 64 (over z, x, core), tensor: 4 (over y).
Axes of the slice: x: 4, y: 4, z: 8, core: 2. Of those that a mesh axis runs over, the one named last changes fastest.
Arguments:
- inputs: bfloat16 [65536, 6144], P('dp'), may hold values from -6 to 6
- pre_act: bfloat16 [65536, 1024], P('dp', 'tensor'), may hold values from -6 to 6
- grad_hidden: bfloat16 [65536, 1024], P('dp', 'tensor'), may hold values from -6 to 6
- master: float32 [6144, 1024], P('dp', 'tensor'), may hold values from -0.1875 to 0.1875
- moment_one: float32 [6144, 1024], P('dp', 'tensor'), may hold values from -6 to 6
- moment_two: float32 [6144, 1024], P('dp', 'tensor'), may hold values from 1 to 262144
Outputs:
- grad_input: bfloat16 [65536, 6144], P('dp', 'tensor')
- new_master: float32 [6144, 1024], P('dp', 'tensor')
- new_one: float32 [6144, 1024], P('dp', 'tensor')
- new_two: float32 [6144, 1024], P('dp', 'tensor')
- new_weights: bfloat16 [6144, 1024], P(None, 'tensor')
All inputs are finite; a program needn't handle non-finite values.
Results may differ from a plain program's by a relative error of at most 0.013.
Values may be sent and summed in bfloat16 or wider, within the bound.
No kernel may reach another device: no remote copies, remote signals or barrier semaphores. Data moves between devices by JAX's collectives and lax.ppermute only.
A program may use at most 128 MiB of HBM per device.

v0:
```python
import math
import jax
import jax.numpy as jnp
from jax import lax
from jax.sharding import PartitionSpec as P

QBLOCK = 256
ADAM_STEP = 10


def gelu_slope(value):
    cdf = 0.5 * (1.0 + jax.scipy.special.erf(value / math.sqrt(2.0)))
    pdf = jnp.exp(-0.5 * value * value) / math.sqrt(2.0 * math.pi)
    return cdf + value * pdf


def encode(term):
    rows, cols = term.shape
    blocks = term.reshape(rows, cols // QBLOCK, QBLOCK)
    scale = (jnp.max(jnp.abs(blocks), axis=2) + 1e-06) / 127.0
    codes = jnp.clip(blocks / scale[:, :, None], -127.0, 127.0).astype(jnp.bfloat16)
    return (codes.reshape(rows, cols), scale)


def decode(codes, scale):
    rows, cols = codes.shape
    blocks = codes.astype(jnp.float32).reshape(rows, cols // QBLOCK, QBLOCK)
    return (blocks * scale[:, :, None]).reshape(rows, cols)


def local(inputs, pre_act, grad_hidden, master, moment_one, moment_two):
    act_grad = (grad_hidden.astype(jnp.float32) * gelu_slope(pre_act.astype(jnp.float32))).astype(
        jnp.bfloat16
    )
    weights = master.astype(jnp.bfloat16)
    terms = jnp.einsum(
        "th,dh->td",
        act_grad,
        lax.all_gather(weights, "dp", axis=0, tiled=True),
        preferred_element_type=jnp.float32,
    )
    grad_input = lax.psum_scatter(
        terms.astype(jnp.bfloat16), "tensor", scatter_dimension=1, tiled=True
    )
    term = jnp.einsum("tr,th->rh", inputs, act_grad, preferred_element_type=jnp.float32)
    codes, scale = encode(term)
    grad = lax.psum_scatter(decode(codes, scale), "dp", scatter_dimension=0, tiled=True)
    new_one = 0.9 * moment_one + 0.1 * grad
    new_two = 0.999 * moment_two + 0.001 * grad * grad
    corr_one = 1.0 - 0.9**ADAM_STEP
    corr_two = 1.0 - 0.999**ADAM_STEP
    update = new_one / corr_one / (jnp.sqrt(new_two / corr_two) + 1e-08) + 0.01 * master
    new_master = master - 0.01 * update
    new_weights = lax.all_gather(new_master.astype(jnp.bfloat16), "dp", axis=0, tiled=True)
    return (grad_input, new_master, new_one, new_two, new_weights)


def solution(mesh):
    in_specs = (
        P("dp", None),
        P("dp", "tensor"),
        P("dp", "tensor"),
        P("dp", "tensor"),
        P("dp", "tensor"),
        P("dp", "tensor"),
    )
    out_specs = (
        P("dp", "tensor"),
        P("dp", "tensor"),
        P("dp", "tensor"),
        P("dp", "tensor"),
        P(None, "tensor"),
    )
    return jax.shard_map(local, mesh=mesh, in_specs=in_specs, out_specs=out_specs, check_vma=False)
```

profile of v0, /device:TPU:1, one launch (start us, length us, event | category | flops | bytes accessed | tf_op | source)
XLA Modules:
  0.0 464.7 jit_solution(8532754055390767680)
XLA Ops:
  7.2 0.0 reduce-scatter.7.cloned.1.call-start
  7.2 7.5 %abs_reduce_fusion = (f32[6144]{0:T(1024)S(1)}, f32[256,6144]{1,0:T(8,128)S(1)}) fusion(bf16[1024,6144]{1,0:T(8,128)(2,1)} %param.6, bf16[1024,256]{1,0:T(8,128)(2,1)} %param.7, bf16[1024,256]{1,0:T(8,128)(2,1)} %param.8), kind=kOutput, calls=%fused_computation.3 | convolution fusion | flops 3227510784 | bytes 19947520 | tf_op jit(solution)/shard_map/tr,th->rh/dot_general | solution.py:45
  14.7 3.6 multiply_bitcast_fusion
  18.3 6.6 %copy.30 = f32[6144,256]{1,0:T(8,128)} copy(f32[6144,256]{0,1:T(8,128)} %multiply_bitcast_fusion) | data formatting | bytes 12582912
  24.9 0.0 copy-start.2
  24.9 0.0 copy-start.3
  24.9 0.0 copy-start.4
  24.9 0.0 copy-start
  24.9 0.0 copy-start.1
  24.9 0.0 reduce-scatter.7.cloned.1.call-update
  24.9 0.0 all-gather.3.cloned.1.call-start
  25.0 146.7 %reduce-scatter.7.cloned.1.call-done = f32[96,256]{1,0:T(8,128)} async-done(((f32[6144,256]{1,0:T(8,128)}), f32[96,256]{1,0:T(8,128)}) %reduce-scatter.7.cloned.1.call-update) | async-done | bytes 98320 | tf_op jit(solution)/shard_map/reduce_scatter | solution.py:47
  171.7 0.0 copy-done.2
  171.7 0.0 copy-done.3
  171.7 0.0 copy-done.4
  171.7 1.7 fusion.12
  173.3 0.0 all-gather.3.cloned.1.call-update
  173.4 0.0 all-gather.5.cloned.1.call-start
  173.4 0.7 all-gather.5.cloned.1.call-update
  174.1 0.0 reduce-scatter.5.cloned.1.call-start
  174.1 83.3 %all-gather.3.cloned.1.call-done = bf16[6144,256]{1,0:T(8,128)(2,1)} async-done(((bf16[96,256]{1,0:T(8,128)(2,1)}), bf16[6144,256]{1,0:T(8,128)(2,1)}) %all-gather.3.cloned.1.call-update) | async-done | bytes 3145744 | tf_op jit(solution)/shard_map/all_gather | solution.py:39
  257.4 0.0 copy-done
  257.4 0.0 copy-done.1
  257.4 8.4 %convolution_convert_fusion = bf16[1024,6144]{1,0:T(8,128)(2,1)} fusion(bf16[6144,256]{1,0:T(8,128)(2,1)} %all-gather.3.cloned.1.call-done, bf16[1024,256]{1,0:T(8,128)(2,1)S(1)} %copy-done, bf16[1024,256]{1,0:T(8,128)(2,1)S(1)} %copy-done.1), kind=kOutput, calls=%fused_computation | convolution fusion | flops 3230662656 | bytes 16777216 | tf_op jit(solution)/shard_map/th,dh->td/dot_general | solution.py:36
  265.8 0.0 reduce-scatter.5.cloned.1.call-update
  265.9 71.1 %all-gather.5.cloned.1.call-done = bf16[6144,256]{1,0:T(8,128)(2,1)} async-done(((bf16[96,256]{1,0:T(8,128)(2,1)}), bf16[6144,256]{1,0:T(8,128)(2,1)}) %all-gather.5.cloned.1.call-update) | async-done | bytes 3145744 | tf_op jit(solution)/shard_map/all_gather | solution.py:54
  336.9 117.5 %reduce-scatter.5.cloned.1.call-done = bf16[1024,1536]{1,0:T(8,128)(2,1)} async-done(((bf16[1024,6144]{1,0:T(8,128)(2,1)}), bf16[1024,1536]{1,0:T(8,128)(2,1)}) %reduce-scatter.5.cloned.1.call-update) | async-done | bytes 3145744 | tf_op jit(solution)/shard_map/reduce_scatter | solution.py:42
  454.4 3.8 copy.33
  (1 shorter events, 0.0 us)
Async XLA Ops:
  7.2 164.5 %reduce-scatter.7.cloned.1.call-start = ((), (), s32[]{:S(2)}) async-start(), calls=%async_computation.5 | async-start | bytes 6389760 | tf_op jit(solution)/shard_map/reduce_scatter | solution.py:47
  24.9 146.8 %copy-start.2 = (f32[96,256]{1,0:T(8,128)S(1)}, f32[96,256]{1,0:T(8,128)}, u32[]{:S(2)}) copy-start(f32[96,256]{1,0:T(8,128)} %param.9) | copy-start | bytes 294916
  24.9 146.8 %copy-start.3 = (f32[96,256]{1,0:T(8,128)S(1)}, f32[96,256]{1,0:T(8,128)}, u32[]{:S(2)}) copy-start(f32[96,256]{1,0:T(8,128)} %param.10) | copy-start | bytes 294916
  24.9 146.8 %copy-start.4 = (f32[96,256]{1,0:T(8,128)S(1)}, f32[96,256]{1,0:T(8,128)}, u32[]{:S(2)}) copy-start(f32[96,256]{1,0:T(8,128)} %param.11) | copy-start | bytes 294916
  24.9 232.5 %copy-start = (bf16[1024,256]{1,0:T(8,128)(2,1)S(1)}, bf16[1024,256]{1,0:T(8,128)(2,1)}, u32[]{:S(2)}) copy-start(bf16[1024,256]{1,0:T(8,128)(2,1)} %param.7) | copy-start | bytes 1572868
  24.9 232.5 %copy-start.1 = (bf16[1024,256]{1,0:T(8,128)(2,1)S(1)}, bf16[1024,256]{1,0:T(8,128)(2,1)}, u32[]{:S(2)}) copy-start(bf16[1024,256]{1,0:T(8,128)(2,1)} %param.8) | copy-start | bytes 1572868
  24.9 232.5 %all-gather.3.cloned.1.call-start = ((), (), s32[]{:S(2)}) async-start(), calls=%async_computation.2 | async-start | bytes 3194880 | tf_op jit(solution)/shard_map/all_gather | solution.py:39
  173.4 163.6 %all-gather.5.cloned.1.call-start = ((), (), s32[]{:S(2)}) async-start(), calls=%async_computation.4 | async-start | bytes 3194880 | tf_op jit(solution)/shard_map/all_gather | solution.py:54
  174.1 280.3 %reduce-scatter.5.cloned.1.call-start = ((), (), s32[]{:S(2)}) async-start(), calls=%async_computation.3 | async-start | bytes 15728640 | tf_op jit(solution)/shard_map/reduce_scatter | solution.py:42
Sparse Core Ops, SparseCore 0:
  25.0 146.5 reduce-scatter.6
  175.4 81.9 all-gather.2
  261.1 75.7 all-gather.4
  340.1 114.1 reduce-scatter.4
where the time goes:
time: 465 us
  waiting for transfers between devices  419 us (90%)
  matrix products  15.9 us (3%)
  between operations  13.8 us (3%)
  local copies, waits for them, and re-layouts  10.4 us (2%)
  other arithmetic  5.24 us (1%)
    reduce_scatter x1, waiting for transfers between devices, local(): lax.psum_scatter(decode(codes, scale), 'dp', scatter_dimension=0, tiled=T...  147 us
    reduce_scatter x1, waiting for transfers between devices, local(): lax.psum_scatter(terms.astype(jnp.bfloat16), 'tensor', scatter_dimension=...  117 us
    all_gather x1, waiting for transfers between devices, local(): lax.all_gather(weights, 'dp', axis=0, tiled=True)  83.3 us
    all_gather x1, waiting for transfers between devices, local(): lax.all_gather(new_master.astype(jnp.bfloat16), 'dp', axis=0, tiled=True)  71.1 us
    unnamed x12, local copies, waits for them, and re-layouts  10.4 us
  transfers between devices with their start and end apart: 4, of which 4 were waited for; matrix products, arithmetic and copies ran while one was open for 2% of the time, Pallas kernels for 0%

commit v1 on v0

--- a/solution.py
+++ b/solution.py
@@ -36,7 +36,9 @@
     terms = jnp.einsum(
         "th,dh->td",
         act_grad,
-        lax.all_gather(weights, "dp", axis=0, tiled=True),
+        jnp.concatenate(
+            lax.all_to_all(jnp.stack([weights] * lax.axis_size("dp")), "dp", 0, 0), axis=0
+        ),
         preferred_element_type=jnp.float32,
     )
     grad_input = lax.psum_scatter(

time: 465 us -> 410 us (0.88)
  waiting for transfers between devices: 419 us -> 350 us
  starting transfers between devices: 0.16 us -> 12.8 us
    all_gather x1 -> x0, waiting for transfers between devices: 83.3 us -> none  [local(): lax.all_gather(weights, 'dp', axis=0, tiled=True)]
    all_to_all x0 -> x1, waiting for transfers between devices: none -> 75.6 us  [local(): lax.all_to_all(jnp.stack([weights] * lax.axis_size('dp')), 'dp', 0, 0)]
    all_gather x1, waiting for transfers between devices: 71.1 us -> 8.39 us  [local(): lax.all_gather(new_master.astype(jnp.bfloat16), 'dp', axis=0, tiled=True)]
    all_to_all x0 -> x1, starting transfers between devices: none -> 12.7 us  [local(): lax.all_to_all(jnp.stack([weights] * lax.axis_size('dp')), 'dp', 0, 0)]
    unnamed x12 -> x8, local copies, waits for them, and re-layouts: 10.4 us -> 10.3 us
where the time goes in v1:
time: 410 us; the launch traced here: 409 us
  waiting for transfers between devices  350 us (85%)
  matrix products  15.5 us (4%)
  between operations  13.8 us (3%)
  starting transfers between devices  12.8 us (3%)
  local copies, waits for them, and re-layouts  12.4 us (3%)
  other arithmetic  5.2 us (1%)
    reduce_scatter x1, waiting for transfers between devices, local(): lax.psum_scatter(decode(codes, scale), 'dp', scatter_dimension=0, tiled=T...  146 us
    reduce_scatter x1, waiting for transfers between devices, local(): lax.psum_scatter(terms.astype(jnp.bfloat16), 'tensor', scatter_dimension=...  119 us
    all_to_all x1, waiting for transfers between devices, local(): lax.all_to_all(jnp.stack([weights] * lax.axis_size('dp')), 'dp', 0, 0)  75.6 us
    all_to_all x1, starting transfers between devices, local(): lax.all_to_all(jnp.stack([weights] * lax.axis_size('dp')), 'dp', 0, 0)  12.7 us
    unnamed x8, local copies, waits for them, and re-layouts  10.3 us
    all_gather x1, waiting for transfers between devices, local(): lax.all_gather(new_master.astype(jnp.bfloat16), 'dp', axis=0, tiled=True)  8.39 us
  transfers between devices with their start and end apart: 4, of which 4 were waited for; matrix products, arithmetic and copies ran while one was open for 2% of the time, Pallas kernels for 0%

profile of v1, /device:TPU:1, one launch (start us, length us, event | category | flops | bytes accessed | tf_op | source)
XLA Modules:
  0.0 409.5 jit_solution(15039876902489215967)
XLA Ops:
  7.2 0.0 reduce-scatter.7.cloned.1.call-start
  7.2 7.5 %abs_reduce_fusion = (f32[6144]{0:T(1024)S(1)}, f32[256,6144]{1,0:T(8,128)S(1)}) fusion(bf16[1024,6144]{1,0:T(8,128)(2,1)} %param.6, bf16[1024,256]{1,0:T(8,128)(2,1)} %param.7, bf16[1024,256]{1,0:T(8,128)(2,1)} %param.8), kind=kOutput, calls=%fused_computation.3 | convolution fusion | flops 3227510784 | bytes 19947520 | tf_op jit(solution)/shard_map/tr,th->rh/dot_general | solution.py:47
  14.7 3.5 multiply_bitcast_fusion
  18.2 6.6 %copy.30 = f32[6144,256]{1,0:T(8,128)} copy(f32[6144,256]{0,1:T(8,128)} %multiply_bitcast_fusion) | data formatting | bytes 12582912
  24.8 0.0 copy-start
  24.8 0.0 copy-start.1
  24.8 0.0 copy-start.2
  24.8 0.0 reduce-scatter.7.cloned.1.call-update
  24.8 146.4 %reduce-scatter.7.cloned.1.call-done = f32[96,256]{1,0:T(8,128)} async-done(((f32[6144,256]{1,0:T(8,128)}), f32[96,256]{1,0:T(8,128)}) %reduce-scatter.7.cloned.1.call-update) | async-done | bytes 98320 | tf_op jit(solution)/shard_map/reduce_scatter | solution.py:49
  171.3 0.0 copy-done
  171.3 0.0 copy-done.1
  171.3 0.0 copy-done.2
  171.3 1.7 fusion.12
  172.9 2.0 stack.2
  175.0 12.7 %all-to-all-start = ((bf16[64,96,256]{2,1,0:T(8,128)(2,1)}), bf16[64,96,256]{2,1,0:T(8,128)(2,1)S(1)}, u32[]{:S(2)}, u32[]{:S(2)}) async-start(bf16[64,96,256]{2,1,0:T(8,128)(2,1)} %stack.2), calls=%async_computation | async-start | bytes 6291456 | tf_op jit(solution)/shard_map/all_to_all | solution.py:40
  187.6 0.0 all-gather.2.cloned.1.call-start
  187.7 0.7 all-gather.2.cloned.1.call-update
  188.4 0.0 reduce-scatter.5.cloned.1.call-start
  188.4 75.6 %all-to-all-done = bf16[64,96,256]{2,1,0:T(8,128)(2,1)S(1)} async-done(((bf16[64,96,256]{2,1,0:T(8,128)(2,1)}), bf16[64,96,256]{2,1,0:T(8,128)(2,1)S(1)}, u32[]{:S(2)}, u32[]{:S(2)}) %all-to-all-start) | async-done | bytes 3145760 | tf_op jit(solution)/shard_map/all_to_all | solution.py:40
  264.0 8.1 %convolution_convert_fusion = bf16[1024,6144]{1,0:T(8,128)(2,1)} fusion(bf16[6144,256]{1,0:T(8,128)(2,1)S(1)} %bitcast.6, bf16[1024,256]{1,0:T(8,128)(2,1)} %param.7, bf16[1024,256]{1,0:T(8,128)(2,1)} %param.8), kind=kOutput, calls=%fused_computation | convolution fusion | flops 3230662656 | bytes 16777216 | tf_op jit(solution)/shard_map/th,dh->td/dot_general | solution.py:36
  272.1 0.0 reduce-scatter.5.cloned.1.call-update
  272.1 8.4 %all-gather.2.cloned.1.call-done = bf16[6144,256]{1,0:T(8,128)(2,1)} async-done(((bf16[96,256]{1,0:T(8,128)(2,1)}), bf16[6144,256]{1,0:T(8,128)(2,1)}) %all-gather.2.cloned.1.call-update) | async-done | bytes 3145744 | tf_op jit(solution)/shard_map/all_gather | solution.py:56
  280.5 118.7 %reduce-scatter.5.cloned.1.call-done = bf16[1024,1536]{1,0:T(8,128)(2,1)} async-done(((bf16[1024,6144]{1,0:T(8,128)(2,1)}), bf16[1024,1536]{1,0:T(8,128)(2,1)}) %reduce-scatter.5.cloned.1.call-update) | async-done | bytes 3145744 | tf_op jit(solution)/shard_map/reduce_scatter | solution.py:44
  399.2 3.8 copy.33
  (1 shorter events, 0.0 us)
Async XLA Ops:
  7.2 164.1 %reduce-scatter.7.cloned.1.call-start = ((), (), s32[]{:S(2)}) async-start(), calls=%async_computation.5 | async-start | bytes 6389760 | tf_op jit(solution)/shard_map/reduce_scatter | solution.py:49
  24.8 146.4 %copy-start = (f32[96,256]{1,0:T(8,128)S(1)}, f32[96,256]{1,0:T(8,128)}, u32[]{:S(2)}) copy-start(f32[96,256]{1,0:T(8,128)} %param.9) | copy-start | bytes 294916
  24.8 146.4 %copy-start.1 = (f32[96,256]{1,0:T(8,128)S(1)}, f32[96,256]{1,0:T(8,128)}, u32[]{:S(2)}) copy-start(f32[96,256]{1,0:T(8,128)} %param.10) | copy-start | bytes 294916
  24.8 146.4 %copy-start.2 = (f32[96,256]{1,0:T(8,128)S(1)}, f32[96,256]{1,0:T(8,128)}, u32[]{:S(2)}) copy-start(f32[96,256]{1,0:T(8,128)} %param.11) | copy-start | bytes 294916
  175.0 89.1 %all-to-all-start = ((bf16[64,96,256]{2,1,0:T(8,128)(2,1)}), bf16[64,96,256]{2,1,0:T(8,128)(2,1)S(1)}, u32[]{:S(2)}, u32[]{:S(2)}) async-start(bf16[64,96,256]{2,1,0:T(8,128)(2,1)} %stack.2), calls=%async_computation | async-start | bytes 6291456 | tf_op jit(solution)/shard_map/all_to_all | solution.py:40
  187.6 92.9 %all-gather.2.cloned.1.call-start = ((), (), s32[]{:S(2)}) async-start(), calls=%async_computation.4 | async-start | bytes 3194880 | tf_op jit(solution)/shard_map/all_gather | solution.py:56
  188.4 210.8 %reduce-scatter.5.cloned.1.call-start = ((), (), s32[]{:S(2)}) async-start(), calls=%async_computation.3 | async-start | bytes 15728640 | tf_op jit(solution)/shard_map/reduce_scatter | solution.py:44
Sparse Core Ops, SparseCore 0:
  25.0 146.2 reduce-scatter.6
  192.2 88.2 all-gather.1
  283.9 115.2 reduce-scatter.4
